TPU v7x, 32 devices: a whole 2x2x4 slice. The times are simulated.
32 devices in a mesh: gx: 4 (over y, x), gy: 8 (over z, core).
Axes of the slice: x: 2, y: 2, z: 4, core: 2. Of those that a mesh axis runs over, the one named last changes fastest.
Arguments:
- e_field: float32 [3, 32, 256, 512], P(None, 'gx', 'gy'), may hold values from -6 to 6
- h_field: float32 [3, 32, 256, 512], P(None, 'gx', 'gy'), may hold values from -6 to 6
- polar: float32 [3, 32, 256, 512], P(None, 'gx', 'gy'), may hold values from -6 to 6
- polar_prev: float32 [3, 32, 256, 512], P(None, 'gx', 'gy'), may hold values from -6 to 6
- material: int32 [32, 256, 512], P('gx', 'gy'), may hold values from 0 to 3
- eps_table: float32 [4], replicated, may hold values from 1 to 6
- delta_table: float32 [4], replicated, may hold values from 0.5 to 4
- omega_table: float32 [4], replicated, may hold values from 0.2 to 1.2
- damping_table: float32 [4], replicated, may hold values from 0.02 to 0.6
- surface_flags: int32 [4, 8], P('gx', 'gy'), may hold values 0 or 1
Outputs:
- e_out: float32 [3, 32, 256, 512], P(None, 'gx', 'gy')
- h_out: float32 [3, 32, 256, 512], P(None, 'gx', 'gy')
- polar_out: float32 [3, 32, 256, 512], P(None, 'gx', 'gy')
- far_field: float32 [2, 2, 4, 16384], replicated
All inputs are finite; a program needn't handle non-finite values. No bound on the sum of `surface_flags` on one device may be relied on, other than what follows from the above.
Results may differ from a plain program's by a relative error of at most 0.0003.
Values sent between devices are 32-bit elements; how exact they have to be, the bound alone decides.
A program may use at most 256 MiB of HBM per device.

v0:
```python
import math
import jax
import jax.numpy as jnp
from jax import lax
from jax.sharding import PartitionSpec as P

NTH = 64
NPH = 256
NDIR = 16384
ZS = 384
DT = 0.55
WAVELENGTHS = (5.0, 4.0)


def shifted(shard, axis, by):
    peers = lax.axis_size(axis)
    pairs = [(i, i + by) for i in range(peers) if 0 <= i + by < peers]
    return lax.ppermute(shard, axis, pairs)


def ahead(field, plane, axis):
    rest = lax.slice_in_dim(field, 1, field.shape[axis], axis=axis)
    return jnp.concatenate([rest, plane], axis=axis) - field


def behind(field, plane, axis):
    rest = lax.slice_in_dim(field, 0, field.shape[axis] - 1, axis=axis)
    return field - jnp.concatenate([plane, rest], axis=axis)


def zero_plane(field, axis):
    shape = list(field.shape)
    shape[axis] = 1
    return jnp.zeros(shape, jnp.float32)


def coefficients(eps_table, delta_table, omega_table, damping_table):
    half = damping_table * (DT / 2.0)
    denom = 1.0 + half
    square = omega_table * omega_table * (DT * DT)
    return (
        (2.0 - square) / denom,
        (half - 1.0) / denom,
        delta_table * square / denom,
        1.0 / eps_table,
    )


def curl_e(ex, ey, ez, xnext, ynext):
    zplane = zero_plane(ex, 2)
    curl_x = ahead(ez, ynext[1], 1) - ahead(ey, zplane, 2)
    curl_y = ahead(ex, zplane, 2) - ahead(ez, xnext[1], 0)
    curl_z = ahead(ey, xnext[0], 0) - ahead(ex, ynext[0], 1)
    return (curl_x, curl_y, curl_z)


def curl_h(hx, hy, hz, xprev, yprev):
    zplane = zero_plane(hx, 2)
    curl_x = behind(hz, yprev[1], 1) - behind(hy, zplane, 2)
    curl_y = behind(hx, zplane, 2) - behind(hz, xprev[1], 0)
    curl_z = behind(hy, xprev[0], 0) - behind(hx, yprev[0], 1)
    return (curl_x, curl_y, curl_z)


def directions(start, count):
    index = start + jnp.arange(count, dtype=jnp.int32)
    theta = ((index // NPH).astype(jnp.float32) + 0.5) * (math.pi / 2.0 / NTH)
    phi = ((index % NPH).astype(jnp.float32) + 0.5) * (2.0 * math.pi / NPH)
    return (jnp.sin(theta) * jnp.cos(phi), jnp.sin(theta) * jnp.sin(phi))


def lookup(material, table, count):
    result = jnp.zeros(material.shape, jnp.float32)
    for index in range(count):
        result = result + jnp.where(material == index, table[index], 0.0)
    return result


def next_planes(ex, ey, ez):
    xface = shifted(jnp.stack([ey[:1], ez[:1]]), "gx", -1)
    yface = shifted(jnp.stack([ex[:, :1], ez[:, :1]]), "gy", -1)
    return ((xface[0], xface[1]), (yface[0], yface[1]))


def prev_planes(hx, hy, hz):
    xface = shifted(jnp.stack([hy[-1:], hz[-1:]]), "gx", 1)
    yface = shifted(jnp.stack([hx[:, -1:], hz[:, -1:]]), "gy", 1)
    return ((xface[0], xface[1]), (yface[0], yface[1]))


def project_cells(real_acc, imag_acc, xvalues, yvalues, start, count):
    rows_x = xvalues.shape[0]
    rows_y = yvalues.shape[0]
    cells = rows_x * rows_y
    real_flat = real_acc.reshape(2, 4, cells)
    imag_flat = imag_acc.reshape(2, 4, cells)
    width = math.gcd(count, 2048)
    blocks = count // width

    def project(offset):
        dir_x, dir_y = directions(start + offset, width)
        parts = []
        for f in range(2):
            wave = 2.0 * math.pi / WAVELENGTHS[f]
            along_x = wave * xvalues[:, None] * dir_x[None, :]
            along_y = wave * yvalues[:, None] * dir_y[None, :]
            cos_x = jnp.cos(along_x)
            sin_x = jnp.sin(along_x)
            cos_y = jnp.cos(along_y)
            sin_y = jnp.sin(along_y)
            cosine = (
                cos_x[:, None, :] * cos_y[None, :, :] - sin_x[:, None, :] * sin_y[None, :, :]
            ).reshape(cells, width)
            sine = (
                sin_x[:, None, :] * cos_y[None, :, :] + cos_x[:, None, :] * sin_y[None, :, :]
            ).reshape(cells, width)
            hi = lax.Precision.HIGHEST
            real_part = jnp.dot(real_flat[f], cosine, precision=hi) - jnp.dot(
                imag_flat[f], sine, precision=hi
            )
            imag_part = jnp.dot(real_flat[f], sine, precision=hi) + jnp.dot(
                imag_flat[f], cosine, precision=hi
            )
            parts.append(jnp.stack([real_part, imag_part]))
        return jnp.stack(parts)

    offsets = jnp.arange(blocks, dtype=jnp.int32) * width
    pieces = lax.map(project, offsets)
    return jnp.moveaxis(pieces, 0, 3).reshape(2, 2, 4, count)


def shards(
    e_field,
    h_field,
    polar,
    polar_prev,
    material,
    eps_table,
    delta_table,
    omega_table,
    damping_table,
    surface_flags,
):
    cells_x = e_field.shape[1]
    cells_y = e_field.shape[2]
    count = eps_table.shape[0]
    coef_a, coef_b, coef_c, coef_inv = coefficients(
        eps_table, delta_table, omega_table, damping_table
    )
    vox_a = lookup(material, coef_a, count)
    vox_b = lookup(material, coef_b, count)
    vox_c = lookup(material, coef_c, count)
    vox_inv = lookup(material, coef_inv, count)
    flag = surface_flags[0, 0].astype(jnp.float32)
    ex, ey, ez = (e_field[0], e_field[1], e_field[2])
    hx, hy, hz = (h_field[0], h_field[1], h_field[2])
    pols = [polar[0], polar[1], polar[2]]
    prevs = [polar_prev[0], polar_prev[1], polar_prev[2]]
    real_acc = jnp.zeros((2, 4, cells_x, cells_y), jnp.float32)
    imag_acc = jnp.zeros((2, 4, cells_x, cells_y), jnp.float32)
    for step in range(2):
        xnext, ynext = next_planes(ex, ey, ez)
        curl_x, curl_y, curl_z = curl_e(ex, ey, ez, xnext, ynext)
        hx = hx - DT * curl_x
        hy = hy - DT * curl_y
        hz = hz - DT * curl_z
        fields = [ex, ey, ez]
        newpol = [vox_a * pols[i] + vox_b * prevs[i] + vox_c * fields[i] for i in range(3)]
        xprev, yprev = prev_planes(hx, hy, hz)
        curls = curl_h(hx, hy, hz, xprev, yprev)
        fields = [fields[i] + (DT * curls[i] - (newpol[i] - pols[i])) * vox_inv for i in range(3)]
        ex, ey, ez = fields
        prevs = pols
        pols = newpol
        surface = jnp.stack([-hy[:, :, ZS], hx[:, :, ZS], ey[:, :, ZS], -ex[:, :, ZS]]) * flag
        moment = (step + 1) * DT
        real_acc = real_acc + jnp.stack(
            [surface * math.cos(2.0 * math.pi / WAVELENGTHS[f] * moment) for f in range(2)]
        )
        imag_acc = imag_acc - jnp.stack(
            [surface * math.sin(2.0 * math.pi / WAVELENGTHS[f] * moment) for f in range(2)]
        )
    xglobal = (lax.axis_index("gx") * cells_x + jnp.arange(cells_x, dtype=jnp.int32)).astype(
        jnp.float32
    )
    yglobal = (lax.axis_index("gy") * cells_y + jnp.arange(cells_y, dtype=jnp.int32)).astype(
        jnp.float32
    )
    partial_far = project_cells(real_acc, imag_acc, xglobal, yglobal, 0, NDIR)
    total = lax.psum(partial_far, ("gx", "gy"))
    grid_x = cells_x * lax.axis_size("gx")
    grid_y = cells_y * lax.axis_size("gy")
    far_field = total * (1.0 / math.sqrt(grid_x * grid_y))
    return (jnp.stack([ex, ey, ez]), jnp.stack([hx, hy, hz]), jnp.stack(pols), far_field)


def solution(mesh):
    placed = (
        P(None, "gx", "gy", None),
        P(None, "gx", "gy", None),
        P(None, "gx", "gy", None),
        P(None, "gx", "gy", None),
        P("gx", "gy", None),
        P(),
        P(),
        P(),
        P(),
        P("gx", "gy"),
    )
    return jax.shard_map(
        shards,
        mesh=mesh,
        in_specs=placed,
        out_specs=(
            P(None, "gx", "gy", None),
            P(None, "gx", "gy", None),
            P(None, "gx", "gy", None),
            P(),
        ),
        check_vma=False,
    )
```

profile of v0, /device:TPU:0, one launch (start us, length us, event | category | flops | bytes accessed | tf_op | source)
XLA Modules:
  0.0 399.2 jit_solution(10119303926188444393)
XLA Ops:
  7.3 1.6 slice_bitcast_fusion.1
  9.0 1.3 collective-permute-start.1
  10.3 1.3 collective-permute-start
  19.7 3.1 fusion.46
  23.1 3.0 collective-permute-start.2
  28.5 6.1 %collective-permute-start.3 = (f32[2,1,32,512]{3,2,1,0:T(8,128)}, f32[2,1,32,512]{3,2,1,0:T(8,128)}, u32[]{:S(2)}, u32[]{:S(2)}) collective-permute-start(f32[2,1,32,512]{3,2,1,0:T(8,128)} %pad_maximum_fusion.3), channel_id=1, source_target_pairs={{0,8},{8,16},{16,24},{1,9},{9,17},{17,25},{2,10},{10,18},{18,26},{... | collective-permute-start | bytes 393224 | tf_op jit(solution)/shard_map/ppermute | solution.py:18
  35.9 13.2 %fusion.51 = (f32[8,32,512]{2,1,0:T(8,128)S(1)}, f32[8,32,512]{2,1,0:T(8,128)}, pred[8,32,512]{2,1,0:T(8,128)(4,1)S(1)}, pred[8,32,512]{2,1,0:T(8,128)(4,1)S(1)}...) fusion(f32[8,32,512]{2,1,0:T(8,128)S(1)} %get-tuple-element.169, f32[8,31,512]{2,1,0:T(8,128)S(1)} %bitcast.335, ...), kind=kLoop, calls=%fused_computation.90 | loop fusion | flops 6029312 | bytes 5766208 | tf_op jit(solution)/shard_map/add | solution.py:171
  51.7 1.3 stack.241
  54.8 13.0 %fusion.64 = (f32[8,32,512]{2,1,0:T(8,128)S(1)}, f32[8,32,512]{2,1,0:T(8,128)}) fusion(f32[8,32,512]{2,1,0:T(8,128)S(1)} %get-tuple-element.170, f32[7,32,512]{2,1,0:T(8,128)} %slice.432, f32[1,32,512]{2,1,0:T(8,128)S(1)} %get-tuple-element.184, f32[8,32,512]{2,1,0:T(8,128)S(1)} %get-tuple-element.168, f32[8,31,512]{2,1,0:T(8,128)S(1)} %bitcast.328, ...), kind=kLoop, calls=%fused_computation.106 | loop fusion | flops 5636096 | bytes 5242944 | tf_op jit(solution)/shard_map/add | solution.py:171
  68.7 12.8 %fusion.59 = (f32[8,32,512]{2,1,0:T(8,128)S(1)}, f32[8,32,512]{2,1,0:T(8,128)}) fusion(f32[8,32,512]{2,1,0:T(8,128)S(1)} %get-tuple-element.169, f32[7,32,512]{2,1,0:T(8,128)S(1)} %copy-done.22, f32[1,32,512]{2,1,0:T(8,128)S(1)} %get-tuple-element.183, f32[8,32,512]{2,1,0:T(8,128)S(1)} %get-tuple-element.168, f32[8,32,511]{2,1,0:T(8,128)S(1)} %bitcast.329, ...), kind=kLoop, calls=%fused_computation.100 | loop fusion | flops 5505024 | bytes 5241920 | tf_op jit(solution)/shard_map/add | solution.py:171
  82.5 1.4 collective-permute-start.5
  85.6 1.3 slice.441
  86.8 1.2 slice.443
  88.2 1.3 collective-permute-start.4
  89.5 5.8 %collective-permute-done.4 = f32[2,1,32,512]{3,2,1,0:T(8,128)S(1)} collective-permute-done((f32[2,1,32,512]{3,2,1,0:T(8,128)S(1)}, f32[2,1,32,512]{3,2,1,0:T(8,128)S(1)}, u32[]{:S(2)}, u32[]{:S(2)}) %collective-permute-start.4) | collective-permute-done | bytes 131104 | tf_op jit(solution)/shard_map/ppermute | solution.py:18
  96.5 2.9 collective-permute-start.6
  99.4 1.3 pad_maximum_fusion.1
  102.3 4.8 %collective-permute-start.7 = (f32[2,1,32,512]{3,2,1,0:T(8,128)S(1)}, f32[2,1,32,512]{3,2,1,0:T(8,128)S(1)}, u32[]{:S(2)}, u32[]{:S(2)}) collective-permute-start(f32[2,1,32,512]{3,2,1,0:T(8,128)S(1)} %pad_maximum_fusion.5), channel_id=1, source_target_pairs={{0,8},{8,16},{16,24},{1,9},{9,17},{17,25},{2,10},{10,18},{18,26},{... | collective-permute-start | bytes 393224 | tf_op jit(solution)/shard_map/ppermute | solution.py:18
  107.3 12.9 %fusion.75 = (f32[8,32,512]{2,1,0:T(8,128)S(1)}, f32[8,32,512]{2,1,0:T(8,128)}) fusion(f32[8,32,512]{2,1,0:T(8,128)S(1)} %copy-done.3, f32[8,32,512]{2,1,0:T(8,128)S(1)} %get-tuple-element.177, f32[8,31,512]{2,1,0:T(8,128)S(1)} %bitcast.334, f32[8,1,512]{2,1,0:T(1,128)S(1)} %get-tuple-element.187, f32[8,32,512]{2,1,0:T(8,128)} %get-tuple-element.137, ...), kind=kLoop, calls=%fused_computation.122 | loop fusion | flops 5505024 | bytes 5241920 | tf_op jit(solution)/shard_map/add | solution.py:171
  121.3 12.9 %fusion.83 = (f32[8,32,512]{2,1,0:T(8,128)S(1)}, f32[8,32,512]{2,1,0:T(8,128)}) fusion(f32[8,32,512]{2,1,0:T(8,128)S(1)} %copy-done.7, f32[8,32,512]{2,1,0:T(8,128)S(1)} %get-tuple-element.177, f32[7,32,512]{2,1,0:T(8,128)} %slice.456, f32[1,32,512]{2,1,0:T(8,128)S(1)} %get-tuple-element.179, f32[8,32,512]{2,1,0:T(8,128)} %get-tuple-element.143, ...), kind=kLoop, calls=%fused_computation.132 | loop fusion | flops 5505024 | bytes 5241920 | tf_op jit(solution)/shard_map/add | solution.py:171
  135.0 122.4 %while.13 = (s32[]{:T(128)}, f32[8,2,2,4,2048]{4,3,2,1,0:T(4,128)}, s32[8]{0:T(128)S(1)}, f32[2,4,256]{2,1,0:T(4,128)S(1)}, f32[2,4,256]{2,1,0:T(4,128)S(1)}, /*index=5*/s32[]{:T(128)}, s32[]{:T(128)}, s32[]{:T(128)}) while((s32[]{:T(128)}, f32[8,2,2,4,2048]{4,3,2,1,0:T(4,128)}, s32[8]{0:T(128)S(1)}, f32[2,4,256]{2,1,0:T(4,128)S(1)}, ...), condition=%wide.region_1.2_spmd.clone, body=%wide.region_0.1_spmd.clone.sunk | while | flops 207937696 | bytes 28771064 | solution.py:128
  136.4 1.9 multiply_cosine_fusion.6
  140.6 1.2 fusion.167
  141.8 1.2 fusion.168
  143.0 1.2 fusion.169
  146.0 1.2 fusion.171
  147.2 1.2 fusion.172
  148.4 1.2 fusion.173
  151.7 1.9 multiply_cosine_fusion.6
  155.9 1.2 fusion.167
  157.1 1.2 fusion.168
  161.3 1.2 fusion.171
  162.5 1.2 fusion.172
  163.7 1.2 fusion.173
  167.0 1.9 multiply_cosine_fusion.6
  171.2 1.2 fusion.167
  172.4 1.2 fusion.168
  173.6 1.2 fusion.169
  176.6 1.2 fusion.171
  177.8 1.2 fusion.172
  179.0 1.2 fusion.173
  182.3 1.9 multiply_cosine_fusion.6
  186.5 1.2 fusion.167
  187.7 1.2 fusion.168
  188.9 1.2 fusion.169
  193.1 1.2 fusion.172
  197.6 1.9 multiply_cosine_fusion.6
  203.0 1.2 fusion.168
  208.4 1.2 fusion.172
  212.9 1.9 multiply_cosine_fusion.6
  218.3 1.2 fusion.168
  223.7 1.2 fusion.172
  228.2 1.9 multiply_cosine_fusion.6
  233.6 1.2 fusion.168
  239.0 1.2 fusion.172
  243.5 1.9 multiply_cosine_fusion.6
  248.9 1.2 fusion.168
  254.3 1.2 fusion.172
  257.4 2.4 copy.16
  259.9 12.3 %fusion.89 = (f32[1,8,32,512]{3,2,1,0:T(8,128)S(1)}, f32[8,32,512]{2,1,0:T(8,128)S(1)}) fusion(f32[8,32,512]{2,1,0:T(8,128)S(1)} %copy-done.11, f32[8,32,512]{2,1,0:T(8,128)S(1)} %get-tuple-element.178, f32[7,32,512]{2,1,0:T(8,128)} %slice.458, f32[1,32,512]{2,1,0:T(8,128)S(1)} %get-tuple-element.180, f32[8,32,512]{2,1,0:T(8,128)S(1)} %get-tuple-element.176, ...), kind=kLoop, calls=%fused_computation.139 | loop fusion | flops 5636096 | bytes 5242944 | tf_op jit(solution)/shard_map/stack | solution.py:194
  272.2 1.3 pad_maximum_fusion
  273.7 1.3 pad_maximum_fusion.2
  275.0 115.0 %all-reduce.10.cloned.1.call-done = f32[2,2,4,16384]{3,2,1,0:T(4,128)} async-done(((f32[2,2,4,16384]{3,2,1,0:T(4,128)}), f32[2,2,4,16384]{3,2,1,0:T(4,128)}) %all-reduce.10.cloned.1.call-update) | async-done | bytes 1048592 | tf_op jit(solution)/shard_map/psum | solution.py:190
  389.9 2.5 broadcast_multiply_fusion
  (263 shorter events, 96.3 us)
Async XLA Ops:
  7.2 3.1 copy-start
  7.2 5.5 %copy-start.33 = (f32[4]{0:T(128)S(1)}, f32[4]{0:T(128)}, u32[]{:S(2)}) copy-start(f32[4]{0:T(128)} %param.17) | copy-start | bytes 52
  7.2 6.2 %copy-start.30 = (f32[4]{0:T(128)S(1)}, f32[4]{0:T(128)}, u32[]{:S(2)}) copy-start(f32[4]{0:T(128)} %param.19) | copy-start | bytes 52
  7.2 6.1 %copy-start.31 = (f32[4]{0:T(128)S(1)}, f32[4]{0:T(128)}, u32[]{:S(2)}) copy-start(f32[4]{0:T(128)} %param.20) | copy-start | bytes 52
  7.2 6.1 %copy-start.32 = (f32[4]{0:T(128)S(1)}, f32[4]{0:T(128)}, u32[]{:S(2)}) copy-start(f32[4]{0:T(128)} %param.18) | copy-start | bytes 52
  7.2 382.7 %all-reduce.10.cloned.1.call-start = ((), (), s32[]{:S(2)}) async-start(), calls=%async_computation | async-start | bytes 2097152 | tf_op jit(solution)/shard_map/psum | solution.py:190
  9.0 10.7 %collective-permute-start.1 = (f32[2,8,1,512]{3,2,1,0:T(1,128)S(1)}, f32[2,8,1,512]{3,2,1,0:T(1,128)S(1)}, u32[]{:S(2)}, u32[]{:S(2)}) collective-permute-start(f32[2,8,1,512]{3,2,1,0:T(1,128)S(1)} %pad_maximum_fusion.6), channel_id=1, source_target_pairs={{1,0},{2,1},{3,2},{4,3},{5,4},{6,5},{7,6},{9,8},{10,9},{11,10},{12... | collective-permute-start | bytes 98312 | tf_op jit(solution)/shard_map/ppermute | solution.py:18
  10.3 9.4 %collective-permute-start = (f32[2,1,32,512]{3,2,1,0:T(8,128)S(1)}, f32[2,1,32,512]{3,2,1,0:T(8,128)S(1)}, u32[]{:S(2)}, u32[]{:S(2)}) collective-permute-start(f32[2,1,32,512]{3,2,1,0:T(8,128)S(1)} %stack.204), channel_id=1, source_target_pairs={{8,0},{16,8},{24,16},{9,1},{17,9},{25,17},{10,2},{18,10},{26,18},{... | collective-permute-start | bytes 393224 | tf_op jit(solution)/shard_map/ppermute | solution.py:18
  23.1 12.8 %collective-permute-start.2 = (f32[2,8,1,512]{3,2,1,0:T(1,128)S(1)}, f32[2,8,1,512]{3,2,1,0:T(1,128)S(1)}, u32[]{:S(2)}, u32[]{:S(2)}) collective-permute-start(f32[2,8,1,512]{3,2,1,0:T(1,128)S(1)} %pad_maximum_fusion.7), channel_id=1, source_target_pairs={{0,1},{1,2},{2,3},{3,4},{4,5},{5,6},{6,7},{8,9},{9,10},{10,11},{11... | collective-permute-start | bytes 98312 | tf_op jit(solution)/shard_map/ppermute | solution.py:18
  28.5 25.5 %collective-permute-start.3 = (f32[2,1,32,512]{3,2,1,0:T(8,128)}, f32[2,1,32,512]{3,2,1,0:T(8,128)}, u32[]{:S(2)}, u32[]{:S(2)}) collective-permute-start(f32[2,1,32,512]{3,2,1,0:T(8,128)} %pad_maximum_fusion.3), channel_id=1, source_target_pairs={{0,8},{8,16},{16,24},{1,9},{9,17},{17,25},{2,10},{10,18},{18,26},{... | collective-permute-start | bytes 393224 | tf_op jit(solution)/shard_map/ppermute | solution.py:18
  49.1 1.9 copy-start.1
  54.8 13.9 %copy-start.12 = (pred[8,32,512]{2,1,0:T(8,128)(4,1)S(1)}, pred[8,32,512]{2,1,0:T(8,128)(4,1)}, u32[]{:S(2)}) copy-start(pred[8,32,512]{2,1,0:T(8,128)(4,1)} %get-tuple-element.141) | copy-start | bytes 393220
  54.8 13.9 %copy-start.22 = (f32[7,32,512]{2,1,0:T(8,128)S(1)}, f32[7,32,512]{2,1,0:T(8,128)}, u32[]{:S(2)}) copy-start(f32[7,32,512]{2,1,0:T(8,128)} %slice.428) | copy-start | bytes 1376260
  67.9 0.8 copy-start.8
  68.7 16.2 %copy-start.27 = (f32[1,1,256]{2,1,0:T(1,128)S(1)}, f32[1,1,256]{2,1,0:T(1,128)}, u32[]{:S(2)}) copy-start(f32[1,1,256]{2,1,0:T(1,128)} %stack.239) | copy-start | bytes 3076
  68.7 16.2 %copy-start.28 = (f32[1,1,256]{2,1,0:T(1,128)S(1)}, f32[1,1,256]{2,1,0:T(1,128)}, u32[]{:S(2)}) copy-start(f32[1,1,256]{2,1,0:T(1,128)} %stack.238) | copy-start | bytes 3076
  68.7 16.2 %copy-start.29 = (f32[1,1,256]{2,1,0:T(1,128)S(1)}, f32[1,1,256]{2,1,0:T(1,128)}, u32[]{:S(2)}) copy-start(f32[1,1,256]{2,1,0:T(1,128)} %stack.241) | copy-start | bytes 3076
  81.5 0.8 copy-start.4
  81.5 6.6 %copy-start.9 = (f32[8,32,512]{2,1,0:T(8,128)S(1)}, f32[8,32,512]{2,1,0:T(8,128)}, u32[]{:S(2)}) copy-start(f32[8,32,512]{2,1,0:T(8,128)} %copy-done.8) | copy-start | bytes 1572868
  82.5 5.6 %copy-start.5 = (f32[8,32,512]{2,1,0:T(8,128)S(1)}, f32[8,32,512]{2,1,0:T(8,128)}, u32[]{:S(2)}) copy-start(f32[8,32,512]{2,1,0:T(8,128)} %copy-done.4) | copy-start | bytes 1572868
  82.5 7.0 %collective-permute-start.5 = (f32[2,8,1,512]{3,2,1,0:T(1,128)S(1)}, f32[2,8,1,512]{3,2,1,0:T(1,128)S(1)}, u32[]{:S(2)}, u32[]{:S(2)}) collective-permute-start(f32[2,8,1,512]{3,2,1,0:T(1,128)S(1)} %pad_maximum_fusion.8), channel_id=1, source_target_pairs={{1,0},{2,1},{3,2},{4,3},{5,4},{6,5},{7,6},{9,8},{10,9},{11,10},{12... | collective-permute-start | bytes 98312 | tf_op jit(solution)/shard_map/ppermute | solution.py:18
  85.5 9.8 %copy-start.2 = (f32[8,32,512]{2,1,0:T(8,128)S(1)}, f32[8,32,512]{2,1,0:T(8,128)}, u32[]{:S(2)}) copy-start(f32[8,32,512]{2,1,0:T(8,128)} %copy-done.1) | copy-start | bytes 1572868
  85.5 9.8 %copy-start.6 = (f32[8,32,512]{2,1,0:T(8,128)S(1)}, f32[8,32,512]{2,1,0:T(8,128)}, u32[]{:S(2)}) copy-start(f32[8,32,512]{2,1,0:T(8,128)} %copy-done.4) | copy-start | bytes 1572868
  85.5 9.8 %copy-start.10 = (f32[8,32,512]{2,1,0:T(8,128)S(1)}, f32[8,32,512]{2,1,0:T(8,128)}, u32[]{:S(2)}) copy-start(f32[8,32,512]{2,1,0:T(8,128)} %copy-done.8) | copy-start | bytes 1572868
  85.5 9.8 %copy-start.20 = (f32[8,31,512]{2,1,0:T(8,128)S(1)}, f32[8,31,512]{2,1,0:T(8,128)}, u32[]{:S(2)}) copy-start(f32[8,31,512]{2,1,0:T(8,128)} %slice.437) | copy-start | bytes 1523716
  85.6 9.8 %copy-start.21 = (f32[8,32,511]{2,1,0:T(8,128)S(1)}, f32[8,32,511]{2,1,0:T(8,128)}, u32[]{:S(2)}) copy-start(f32[8,32,511]{2,1,0:T(8,128)} %slice.448) | copy-start | bytes 1569796
  88.2 7.1 %collective-permute-start.4 = (f32[2,1,32,512]{3,2,1,0:T(8,128)S(1)}, f32[2,1,32,512]{3,2,1,0:T(8,128)S(1)}, u32[]{:S(2)}, u32[]{:S(2)}) collective-permute-start(f32[2,1,32,512]{3,2,1,0:T(8,128)S(1)} %pad_maximum_fusion.4), channel_id=1, source_target_pairs={{8,0},{16,8},{24,16},{9,1},{17,9},{25,17},{10,2},{18,10},{26,18},{... | collective-permute-start | bytes 393224 | tf_op jit(solution)/shard_map/ppermute | solution.py:18
  96.5 10.8 %collective-permute-start.6 = (f32[2,8,1,512]{3,2,1,0:T(1,128)S(1)}, f32[2,8,1,512]{3,2,1,0:T(1,128)S(1)}, u32[]{:S(2)}, u32[]{:S(2)}) collective-permute-start(f32[2,8,1,512]{3,2,1,0:T(1,128)S(1)} %pad_maximum_fusion.9), channel_id=1, source_target_pairs={{0,1},{1,2},{2,3},{3,4},{4,5},{5,6},{6,7},{8,9},{9,10},{10,11},{11... | collective-permute-start | bytes 98312 | tf_op jit(solution)/shard_map/ppermute | solution.py:18
  99.4 7.9 %copy-start.3 = (f32[8,32,512]{2,1,0:T(8,128)S(1)}, f32[8,32,512]{2,1,0:T(8,128)}, u32[]{:S(2)}) copy-start(f32[8,32,512]{2,1,0:T(8,128)} %copy-done.1) | copy-start | bytes 1572868
  99.4 7.9 %copy-start.13 = (pred[8,32,512]{2,1,0:T(8,128)(4,1)S(1)}, pred[8,32,512]{2,1,0:T(8,128)(4,1)}, u32[]{:S(2)}) copy-start(pred[8,32,512]{2,1,0:T(8,128)(4,1)} %get-tuple-element.141) | copy-start | bytes 393220
  102.3 18.9 %collective-permute-start.7 = (f32[2,1,32,512]{3,2,1,0:T(8,128)S(1)}, f32[2,1,32,512]{3,2,1,0:T(8,128)S(1)}, u32[]{:S(2)}, u32[]{:S(2)}) collective-permute-start(f32[2,1,32,512]{3,2,1,0:T(8,128)S(1)} %pad_maximum_fusion.5), channel_id=1, source_target_pairs={{0,8},{8,16},{16,24},{1,9},{9,17},{17,25},{2,10},{10,18},{18,26},{... | collective-permute-start | bytes 393224 | tf_op jit(solution)/shard_map/ppermute | solution.py:18
  107.3 13.9 %copy-start.7 = (f32[8,32,512]{2,1,0:T(8,128)S(1)}, f32[8,32,512]{2,1,0:T(8,128)}, u32[]{:S(2)}) copy-start(f32[8,32,512]{2,1,0:T(8,128)} %copy-done.4) | copy-start | bytes 1572868
  120.2 0.8 copy-start.14
  121.2 13.2 %copy-start.25 = (f32[1,4,256]{2,1,0:T(4,128)S(1)}, f32[1,4,256]{2,1,0:T(4,128)}, u32[]{:S(2)}) copy-start(f32[1,4,256]{2,1,0:T(4,128)} %get-tuple-element.200) | copy-start | bytes 12292
  121.2 13.2 %copy-start.26 = (f32[1,4,256]{2,1,0:T(4,128)S(1)}, f32[1,4,256]{2,1,0:T(4,128)}, u32[]{:S(2)}) copy-start(f32[1,4,256]{2,1,0:T(4,128)} %get-tuple-element.202) | copy-start | bytes 12292
  121.2 13.2 %copy-start.23 = (f32[1,4,256]{2,1,0:T(4,128)S(1)}, f32[1,4,256]{2,1,0:T(4,128)}, u32[]{:S(2)}) copy-start(f32[1,4,256]{2,1,0:T(4,128)} %get-tuple-element.199) | copy-start | bytes 12292
  121.3 13.2 %copy-start.24 = (f32[1,4,256]{2,1,0:T(4,128)S(1)}, f32[1,4,256]{2,1,0:T(4,128)}, u32[]{:S(2)}) copy-start(f32[1,4,256]{2,1,0:T(4,128)} %get-tuple-element.201) | copy-start | bytes 12292
  121.3 13.2 %copy-start.34 = (s32[8]{0:T(128)S(1)}, s32[8]{0:T(128)}, u32[]{:S(2)}) copy-start(s32[8]{0:T(128)} %iota_multiply_fusion) | copy-start | bytes 100
  134.2 0.8 copy-start.16
  257.4 2.5 copy-start.11
  259.9 12.3 %copy-start.15 = (f32[8,32,512]{2,1,0:T(8,128)S(1)}, f32[8,32,512]{2,1,0:T(8,128)}, u32[]{:S(2)}) copy-start(f32[8,32,512]{2,1,0:T(8,128)} %copy-done.14) | copy-start | bytes 1572868
  259.9 12.3 %copy-start.17 = (f32[8,32,512]{2,1,0:T(8,128)S(1)}, f32[8,32,512]{2,1,0:T(8,128)}, u32[]{:S(2)}) copy-start(f32[8,32,512]{2,1,0:T(8,128)} %copy-done.16) | copy-start | bytes 1572868
  272.2 1.3 copy-start.18
  272.2 1.5 copy-start.19
Sparse Core Ops, SparseCore 0:
  260.0 129.8 all-reduce.9
where the time goes:
time: 401 us; the launch traced here: 399 us
  other arithmetic  132 us (33%)
  waiting for transfers between devices  121 us (30%)
  matrix products  76.3 us (19%)
  local copies, waits for them, and re-layouts  32.3 us (8%)
  starting transfers between devices  22.1 us (6%)
  between operations  15.5 us (4%)
    psum x1, waiting for transfers between devices, shards(): total = lax.psum(partial_far, ('gx', 'gy'))  115 us
    add x5, other arithmetic, shards(): fields[i] + (DT * curls[i] - (newpol[i] - pols[i])) * vox_inv  64.9 us
    ppermute x8, starting transfers between devices, shifted(): return lax.ppermute(shard, axis, pairs)  22.1 us
    dot_general x16, matrix products, project(): jnp.dot(real_flat[f], cosine, precision=hi)  19.1 us
    dot_general x16, matrix products, project(): jnp.dot(imag_flat[f], cosine, precision=hi)  19.1 us
    dot_general x16, matrix products, project(): jnp.dot(imag_flat[f], sine, precision=hi)  19.1 us
    dot_general x16, matrix products, project(): jnp.dot(real_flat[f], sine, precision=hi)  19 us
    cos x8, other arithmetic, project(): cos_y = jnp.cos(along_y)  15.1 us
  transfers between devices with their start and end apart: 9, of which 2 were waited for; matrix products, arithmetic and copies ran while one was open for 16% of the time, Pallas kernels for 0%

commit v1 on v0

--- a/solution.py
+++ b/solution.py
@@ -187,7 +187,8 @@
         jnp.float32
     )
     partial_far = project_cells(real_acc, imag_acc, xglobal, yglobal, 0, NDIR)
-    total = lax.psum(partial_far, ("gx", "gy"))
+    one_axis = lax.psum(partial_far, "gy")
+    total = lax.psum(one_axis, "gx")
     grid_x = cells_x * lax.axis_size("gx")
     grid_y = cells_y * lax.axis_size("gy")
     far_field = total * (1.0 / math.sqrt(grid_x * grid_y))

time: 401 us -> 382 us (0.953)
  waiting for transfers between devices: 121 us -> 103 us
    psum x1 -> x2, waiting for transfers between devices: 115 us -> 97.3 us  [the longest x1 59 us: shards(): one_axis = lax.psum(partial_far, 'gy')]
  transfers between devices with their start and end apart: 9 -> 10, of which waited for: 2 -> 3; matrix products, arithmetic and copies ran while one was open for 16% -> 17% of each run, Pallas kernels for 0% -> 0%
where the time goes in v1:
time: 382 us; the launch traced here: 380 us
  other arithmetic  132 us (35%)
  waiting for transfers between devices  103 us (27%)
  matrix products  76.3 us (20%)
  local copies, waits for them, and re-layouts  30.5 us (8%)
  starting transfers between devices  22.2 us (6%)
  between operations  15.4 us (4%)
    add x5, other arithmetic, shards(): fields[i] + (DT * curls[i] - (newpol[i] - pols[i])) * vox_inv  65.3 us
    psum x1, waiting for transfers between devices, shards(): one_axis = lax.psum(partial_far, 'gy')  59 us
    psum x1, waiting for transfers between devices, shards(): total = lax.psum(one_axis, 'gx')  38.4 us
    ppermute x8, starting transfers between devices, shifted(): return lax.ppermute(shard, axis, pairs)  22.1 us
    dot_general x16, matrix products, project(): jnp.dot(real_flat[f], cosine, precision=hi)  19.1 us
    dot_general x16, matrix products, project(): jnp.dot(imag_flat[f], sine, precision=hi)  19.1 us
    dot_general x16, matrix products, project(): jnp.dot(imag_flat[f], cosine, precision=hi)  19.1 us
    dot_general x16, matrix products, project(): jnp.dot(real_flat[f], sine, precision=hi)  19 us
  transfers between devices with their start and end apart: 10, of which 3 were waited for; matrix products, arithmetic and copies ran while one was open for 17% of the time, Pallas kernels for 0%

profile of v1, /device:TPU:0, one launch (start us, length us, event | category | flops | bytes accessed | tf_op | source)
XLA Modules:
  0.0 380.4 jit_solution(4233388220097985972)
XLA Ops:
  7.3 1.6 slice_bitcast_fusion.1
  9.0 1.3 collective-permute-start.1
  10.3 1.3 collective-permute-start
  19.7 3.1 fusion.46
  23.1 3.0 collective-permute-start.2
  28.4 6.1 %collective-permute-start.3 = (f32[2,1,32,512]{3,2,1,0:T(8,128)}, f32[2,1,32,512]{3,2,1,0:T(8,128)}, u32[]{:S(2)}, u32[]{:S(2)}) collective-permute-start(f32[2,1,32,512]{3,2,1,0:T(8,128)} %pad_maximum_fusion.3), channel_id=1, source_target_pairs={{0,8},{8,16},{16,24},{1,9},{9,17},{17,25},{2,10},{10,18},{18,26},{... | collective-permute-start | bytes 393224 | tf_op jit(solution)/shard_map/ppermute | solution.py:18
  35.8 13.2 %fusion.51 = (f32[8,32,512]{2,1,0:T(8,128)S(1)}, f32[8,32,512]{2,1,0:T(8,128)}, pred[8,32,512]{2,1,0:T(8,128)(4,1)S(1)}, pred[8,32,512]{2,1,0:T(8,128)(4,1)S(1)}...) fusion(f32[8,32,512]{2,1,0:T(8,128)S(1)} %get-tuple-element.169, f32[8,31,512]{2,1,0:T(8,128)S(1)} %bitcast.335, ...), kind=kLoop, calls=%fused_computation.90 | loop fusion | flops 6029312 | bytes 5766208 | tf_op jit(solution)/shard_map/add | solution.py:171
  51.8 1.3 stack.241
  54.9 13.1 %fusion.64 = (f32[8,32,512]{2,1,0:T(8,128)S(1)}, f32[8,32,512]{2,1,0:T(8,128)}) fusion(f32[8,32,512]{2,1,0:T(8,128)S(1)} %get-tuple-element.170, f32[7,32,512]{2,1,0:T(8,128)} %slice.432, f32[1,32,512]{2,1,0:T(8,128)S(1)} %get-tuple-element.184, f32[8,32,512]{2,1,0:T(8,128)S(1)} %get-tuple-element.168, f32[8,31,512]{2,1,0:T(8,128)S(1)} %bitcast.328, ...), kind=kLoop, calls=%fused_computation.106 | loop fusion | flops 5636096 | bytes 5242944 | tf_op jit(solution)/shard_map/add | solution.py:171
  68.8 12.9 %fusion.59 = (f32[8,32,512]{2,1,0:T(8,128)S(1)}, f32[8,32,512]{2,1,0:T(8,128)}) fusion(f32[8,32,512]{2,1,0:T(8,128)S(1)} %get-tuple-element.169, f32[7,32,512]{2,1,0:T(8,128)S(1)} %copy-done.21, f32[1,32,512]{2,1,0:T(8,128)S(1)} %get-tuple-element.183, f32[8,32,512]{2,1,0:T(8,128)S(1)} %get-tuple-element.168, f32[8,32,511]{2,1,0:T(8,128)S(1)} %bitcast.329, ...), kind=kLoop, calls=%fused_computation.100 | loop fusion | flops 5505024 | bytes 5241920 | tf_op jit(solution)/shard_map/add | solution.py:171
  82.7 1.4 collective-permute-start.5
  85.8 1.3 slice.441
  87.1 1.2 slice.443
  88.4 1.3 collective-permute-start.4
  89.7 5.8 %collective-permute-done.4 = f32[2,1,32,512]{3,2,1,0:T(8,128)S(1)} collective-permute-done((f32[2,1,32,512]{3,2,1,0:T(8,128)S(1)}, f32[2,1,32,512]{3,2,1,0:T(8,128)S(1)}, u32[]{:S(2)}, u32[]{:S(2)}) %collective-permute-start.4) | collective-permute-done | bytes 131104 | tf_op jit(solution)/shard_map/ppermute | solution.py:18
  96.8 2.8 collective-permute-start.6
  100.4 4.8 %collective-permute-start.7 = (f32[2,1,32,512]{3,2,1,0:T(8,128)S(1)}, f32[2,1,32,512]{3,2,1,0:T(8,128)S(1)}, u32[]{:S(2)}, u32[]{:S(2)}) collective-permute-start(f32[2,1,32,512]{3,2,1,0:T(8,128)S(1)} %pad_maximum_fusion.5), channel_id=1, source_target_pairs={{0,8},{8,16},{16,24},{1,9},{9,17},{17,25},{2,10},{10,18},{18,26},{... | collective-permute-start | bytes 393224 | tf_op jit(solution)/shard_map/ppermute | solution.py:18
  105.4 13.1 %fusion.75 = (f32[8,32,512]{2,1,0:T(8,128)S(1)}, f32[8,32,512]{2,1,0:T(8,128)}) fusion(f32[8,32,512]{2,1,0:T(8,128)S(1)} %copy-done.3, f32[8,32,512]{2,1,0:T(8,128)S(1)} %get-tuple-element.177, f32[8,31,512]{2,1,0:T(8,128)S(1)} %bitcast.333, f32[8,1,512]{2,1,0:T(1,128)S(1)} %get-tuple-element.187, f32[8,32,512]{2,1,0:T(8,128)} %get-tuple-element.137, ...), kind=kLoop, calls=%fused_computation.122 | loop fusion | flops 5505024 | bytes 5241920 | tf_op jit(solution)/shard_map/add | solution.py:171
  119.5 13.0 %fusion.83 = (f32[8,32,512]{2,1,0:T(8,128)S(1)}, f32[8,32,512]{2,1,0:T(8,128)}) fusion(f32[8,32,512]{2,1,0:T(8,128)S(1)} %copy-done.7, f32[8,32,512]{2,1,0:T(8,128)S(1)} %get-tuple-element.177, f32[7,32,512]{2,1,0:T(8,128)} %slice.456, f32[1,32,512]{2,1,0:T(8,128)S(1)} %get-tuple-element.179, f32[8,32,512]{2,1,0:T(8,128)} %get-tuple-element.143, ...), kind=kLoop, calls=%fused_computation.132 | loop fusion | flops 5505024 | bytes 5241920 | tf_op jit(solution)/shard_map/add | solution.py:171
  132.8 122.4 %while.13 = (s32[]{:T(128)}, f32[8,2,2,4,2048]{4,3,2,1,0:T(4,128)}, s32[8]{0:T(128)S(1)}, f32[2,4,256]{2,1,0:T(4,128)S(1)}, f32[2,4,256]{2,1,0:T(4,128)S(1)}, /*index=5*/s32[]{:T(128)}, s32[]{:T(128)}, s32[]{:T(128)}) while((s32[]{:T(128)}, f32[8,2,2,4,2048]{4,3,2,1,0:T(4,128)}, s32[8]{0:T(128)S(1)}, f32[2,4,256]{2,1,0:T(4,128)S(1)}, ...), condition=%wide.region_1.2_spmd.clone, body=%wide.region_0.1_spmd.clone.sunk | while | flops 207937696 | bytes 28771064 | solution.py:128
  134.3 1.9 multiply_cosine_fusion.6
  138.5 1.2 fusion.167
  139.7 1.2 fusion.168
  140.9 1.2 fusion.169
  143.9 1.2 fusion.171
  145.1 1.2 fusion.172
  146.3 1.2 fusion.173
  149.6 1.9 multiply_cosine_fusion.6
  153.8 1.2 fusion.167
  155.0 1.2 fusion.168
  156.2 1.2 fusion.169
  159.2 1.2 fusion.171
  160.4 1.2 fusion.172
  161.6 1.2 fusion.173
  164.8 1.9 multiply_cosine_fusion.6
  169.1 1.2 fusion.167
  170.3 1.2 fusion.168
  171.5 1.2 fusion.169
  174.5 1.2 fusion.171
  175.7 1.2 fusion.172
  180.1 1.9 multiply_cosine_fusion.6
  185.5 1.2 fusion.168
  190.9 1.2 fusion.172
  195.4 1.9 multiply_cosine_fusion.6
  200.8 1.2 fusion.168
  206.2 1.2 fusion.172
  210.6 1.9 multiply_cosine_fusion.6
  216.1 1.2 fusion.168
  221.5 1.2 fusion.172
  225.9 1.9 multiply_cosine_fusion.6
  231.3 1.2 fusion.168
  236.7 1.2 fusion.172
  241.2 1.9 multiply_cosine_fusion.6
  246.6 1.2 fusion.168
  252.0 1.2 fusion.172
  253.2 1.2 fusion.173
  255.1 2.3 copy.16
  257.5 59.0 %all-reduce.11.cloned.1.call-done = f32[2,2,4,16384]{3,2,1,0:T(4,128)} async-done(((f32[2,2,4,16384]{3,2,1,0:T(4,128)}), f32[2,2,4,16384]{3,2,1,0:T(4,128)}) %all-reduce.11.cloned.1.call-update) | async-done | bytes 1048592 | tf_op jit(solution)/shard_map/psum | solution.py:190
  316.6 1.3 pad_maximum_fusion.1
  317.9 12.0 %fusion.89 = (f32[1,8,32,512]{3,2,1,0:T(8,128)S(1)}, f32[8,32,512]{2,1,0:T(8,128)S(1)}) fusion(f32[8,32,512]{2,1,0:T(8,128)S(1)} %copy-done.11, f32[8,32,512]{2,1,0:T(8,128)S(1)} %get-tuple-element.178, f32[7,32,512]{2,1,0:T(8,128)S(1)} %slice.458, f32[1,32,512]{2,1,0:T(8,128)S(1)} %get-tuple-element.180, f32[8,32,512]{2,1,0:T(8,128)S(1)} %get-tuple-element.176, ...), kind=kLoop, calls=%fused_computation.139 | loop fusion | flops 5636096 | bytes 5242944 | tf_op jit(solution)/shard_map/stack | solution.py:195
  329.9 1.3 pad_maximum_fusion
  331.4 1.3 pad_maximum_fusion.2
  332.7 38.4 %all-reduce.13.cloned.1.call-done = f32[2,2,4,16384]{3,2,1,0:T(4,128)} async-done(((f32[2,2,4,16384]{3,2,1,0:T(4,128)}), f32[2,2,4,16384]{3,2,1,0:T(4,128)}) %all-reduce.13.cloned.1.call-update) | async-done | bytes 1048592 | tf_op jit(solution)/shard_map/psum | solution.py:191
  371.1 2.5 broadcast_multiply_fusion
  (250 shorter events, 96.1 us)
Async XLA Ops:
  7.2 3.1 copy-start
  7.2 5.5 %copy-start.25 = (f32[4]{0:T(128)S(1)}, f32[4]{0:T(128)}, u32[]{:S(2)}) copy-start(f32[4]{0:T(128)} %param.17) | copy-start | bytes 52
  7.2 6.1 %copy-start.22 = (f32[4]{0:T(128)S(1)}, f32[4]{0:T(128)}, u32[]{:S(2)}) copy-start(f32[4]{0:T(128)} %param.19) | copy-start | bytes 52
  7.2 6.1 %copy-start.23 = (f32[4]{0:T(128)S(1)}, f32[4]{0:T(128)}, u32[]{:S(2)}) copy-start(f32[4]{0:T(128)} %param.20) | copy-start | bytes 52
  7.2 6.1 %copy-start.24 = (f32[4]{0:T(128)S(1)}, f32[4]{0:T(128)}, u32[]{:S(2)}) copy-start(f32[4]{0:T(128)} %param.18) | copy-start | bytes 52
  7.2 309.3 %all-reduce.11.cloned.1.call-start = ((), (), s32[]{:S(2)}) async-start(), calls=%async_computation | async-start | bytes 2097152 | tf_op jit(solution)/shard_map/psum | solution.py:190
  9.0 10.7 %collective-permute-start.1 = (f32[2,8,1,512]{3,2,1,0:T(1,128)S(1)}, f32[2,8,1,512]{3,2,1,0:T(1,128)S(1)}, u32[]{:S(2)}, u32[]{:S(2)}) collective-permute-start(f32[2,8,1,512]{3,2,1,0:T(1,128)S(1)} %pad_maximum_fusion.6), channel_id=1, source_target_pairs={{1,0},{2,1},{3,2},{4,3},{5,4},{6,5},{7,6},{9,8},{10,9},{11,10},{12... | collective-permute-start | bytes 98312 | tf_op jit(solution)/shard_map/ppermute | solution.py:18
  10.3 9.4 %collective-permute-start = (f32[2,1,32,512]{3,2,1,0:T(8,128)S(1)}, f32[2,1,32,512]{3,2,1,0:T(8,128)S(1)}, u32[]{:S(2)}, u32[]{:S(2)}) collective-permute-start(f32[2,1,32,512]{3,2,1,0:T(8,128)S(1)} %stack.204), channel_id=1, source_target_pairs={{8,0},{16,8},{24,16},{9,1},{17,9},{25,17},{10,2},{18,10},{26,18},{... | collective-permute-start | bytes 393224 | tf_op jit(solution)/shard_map/ppermute | solution.py:18
  23.1 12.8 %collective-permute-start.2 = (f32[2,8,1,512]{3,2,1,0:T(1,128)S(1)}, f32[2,8,1,512]{3,2,1,0:T(1,128)S(1)}, u32[]{:S(2)}, u32[]{:S(2)}) collective-permute-start(f32[2,8,1,512]{3,2,1,0:T(1,128)S(1)} %pad_maximum_fusion.7), channel_id=1, source_target_pairs={{0,1},{1,2},{2,3},{3,4},{4,5},{5,6},{6,7},{8,9},{9,10},{10,11},{11... | collective-permute-start | bytes 98312 | tf_op jit(solution)/shard_map/ppermute | solution.py:18
  28.4 25.6 %collective-permute-start.3 = (f32[2,1,32,512]{3,2,1,0:T(8,128)}, f32[2,1,32,512]{3,2,1,0:T(8,128)}, u32[]{:S(2)}, u32[]{:S(2)}) collective-permute-start(f32[2,1,32,512]{3,2,1,0:T(8,128)} %pad_maximum_fusion.3), channel_id=1, source_target_pairs={{0,8},{8,16},{16,24},{1,9},{9,17},{17,25},{2,10},{10,18},{18,26},{... | collective-permute-start | bytes 393224 | tf_op jit(solution)/shard_map/ppermute | solution.py:18
  49.1 2.0 copy-start.1
  54.9 13.9 %copy-start.12 = (pred[8,32,512]{2,1,0:T(8,128)(4,1)S(1)}, pred[8,32,512]{2,1,0:T(8,128)(4,1)}, u32[]{:S(2)}) copy-start(pred[8,32,512]{2,1,0:T(8,128)(4,1)} %get-tuple-element.141) | copy-start | bytes 393220
  54.9 13.9 %copy-start.21 = (f32[7,32,512]{2,1,0:T(8,128)S(1)}, f32[7,32,512]{2,1,0:T(8,128)}, u32[]{:S(2)}) copy-start(f32[7,32,512]{2,1,0:T(8,128)} %slice.428) | copy-start | bytes 1376260
  68.0 0.8 copy-start.8
  81.7 0.8 copy-start.4
  81.7 6.7 %copy-start.9 = (f32[8,32,512]{2,1,0:T(8,128)S(1)}, f32[8,32,512]{2,1,0:T(8,128)}, u32[]{:S(2)}) copy-start(f32[8,32,512]{2,1,0:T(8,128)} %copy-done.8) | copy-start | bytes 1572868
  82.6 5.7 %copy-start.5 = (f32[8,32,512]{2,1,0:T(8,128)S(1)}, f32[8,32,512]{2,1,0:T(8,128)}, u32[]{:S(2)}) copy-start(f32[8,32,512]{2,1,0:T(8,128)} %copy-done.4) | copy-start | bytes 1572868
  82.7 7.0 %collective-permute-start.5 = (f32[2,8,1,512]{3,2,1,0:T(1,128)S(1)}, f32[2,8,1,512]{3,2,1,0:T(1,128)S(1)}, u32[]{:S(2)}, u32[]{:S(2)}) collective-permute-start(f32[2,8,1,512]{3,2,1,0:T(1,128)S(1)} %pad_maximum_fusion.8), channel_id=1, source_target_pairs={{1,0},{2,1},{3,2},{4,3},{5,4},{6,5},{7,6},{9,8},{10,9},{11,10},{12... | collective-permute-start | bytes 98312 | tf_op jit(solution)/shard_map/ppermute | solution.py:18
  85.8 9.8 %copy-start.2 = (f32[8,32,512]{2,1,0:T(8,128)S(1)}, f32[8,32,512]{2,1,0:T(8,128)}, u32[]{:S(2)}) copy-start(f32[8,32,512]{2,1,0:T(8,128)} %copy-done.1) | copy-start | bytes 1572868
  85.8 9.8 %copy-start.6 = (f32[8,32,512]{2,1,0:T(8,128)S(1)}, f32[8,32,512]{2,1,0:T(8,128)}, u32[]{:S(2)}) copy-start(f32[8,32,512]{2,1,0:T(8,128)} %copy-done.4) | copy-start | bytes 1572868
  85.8 9.8 %copy-start.10 = (f32[8,32,512]{2,1,0:T(8,128)S(1)}, f32[8,32,512]{2,1,0:T(8,128)}, u32[]{:S(2)}) copy-start(f32[8,32,512]{2,1,0:T(8,128)} %copy-done.8) | copy-start | bytes 1572868
  85.8 9.8 %copy-start.19 = (f32[8,31,512]{2,1,0:T(8,128)S(1)}, f32[8,31,512]{2,1,0:T(8,128)}, u32[]{:S(2)}) copy-start(f32[8,31,512]{2,1,0:T(8,128)} %slice.437) | copy-start | bytes 1523716
  85.8 9.8 %copy-start.20 = (f32[8,32,511]{2,1,0:T(8,128)S(1)}, f32[8,32,511]{2,1,0:T(8,128)}, u32[]{:S(2)}) copy-start(f32[8,32,511]{2,1,0:T(8,128)} %slice.448) | copy-start | bytes 1569796
  88.4 7.2 %collective-permute-start.4 = (f32[2,1,32,512]{3,2,1,0:T(8,128)S(1)}, f32[2,1,32,512]{3,2,1,0:T(8,128)S(1)}, u32[]{:S(2)}, u32[]{:S(2)}) collective-permute-start(f32[2,1,32,512]{3,2,1,0:T(8,128)S(1)} %pad_maximum_fusion.4), channel_id=1, source_target_pairs={{8,0},{16,8},{24,16},{9,1},{17,9},{25,17},{10,2},{18,10},{26,18},{... | collective-permute-start | bytes 393224 | tf_op jit(solution)/shard_map/ppermute | solution.py:18
  96.4 9.0 %copy-start.3 = (f32[8,32,512]{2,1,0:T(8,128)S(1)}, f32[8,32,512]{2,1,0:T(8,128)}, u32[]{:S(2)}) copy-start(f32[8,32,512]{2,1,0:T(8,128)} %copy-done.1) | copy-start | bytes 1572868
  96.8 8.6 %collective-permute-start.6 = (f32[2,8,1,512]{3,2,1,0:T(1,128)S(1)}, f32[2,8,1,512]{3,2,1,0:T(1,128)S(1)}, u32[]{:S(2)}, u32[]{:S(2)}) collective-permute-start(f32[2,8,1,512]{3,2,1,0:T(1,128)S(1)} %pad_maximum_fusion.9), channel_id=1, source_target_pairs={{0,1},{1,2},{2,3},{3,4},{4,5},{5,6},{6,7},{8,9},{9,10},{10,11},{11... | collective-permute-start | bytes 98312 | tf_op jit(solution)/shard_map/ppermute | solution.py:18
  100.4 19.0 %collective-permute-start.7 = (f32[2,1,32,512]{3,2,1,0:T(8,128)S(1)}, f32[2,1,32,512]{3,2,1,0:T(8,128)S(1)}, u32[]{:S(2)}, u32[]{:S(2)}) collective-permute-start(f32[2,1,32,512]{3,2,1,0:T(8,128)S(1)} %pad_maximum_fusion.5), channel_id=1, source_target_pairs={{0,8},{8,16},{16,24},{1,9},{9,17},{17,25},{2,10},{10,18},{18,26},{... | collective-permute-start | bytes 393224 | tf_op jit(solution)/shard_map/ppermute | solution.py:18
  105.4 14.1 %copy-start.7 = (f32[8,32,512]{2,1,0:T(8,128)S(1)}, f32[8,32,512]{2,1,0:T(8,128)}, u32[]{:S(2)}) copy-start(f32[8,32,512]{2,1,0:T(8,128)} %copy-done.4) | copy-start | bytes 1572868
  105.4 14.1 %copy-start.13 = (pred[8,32,512]{2,1,0:T(8,128)(4,1)S(1)}, pred[8,32,512]{2,1,0:T(8,128)(4,1)}, u32[]{:S(2)}) copy-start(pred[8,32,512]{2,1,0:T(8,128)(4,1)} %get-tuple-element.141) | copy-start | bytes 393220
  118.5 0.8 copy-start.14
  119.5 13.2 %copy-start.26 = (s32[8]{0:T(128)S(1)}, s32[8]{0:T(128)}, u32[]{:S(2)}) copy-start(s32[8]{0:T(128)} %iota_multiply_fusion) | copy-start | bytes 100
  257.5 113.6 %all-reduce.13.cloned.1.call-start = ((), (), s32[]{:S(2)}) async-start(), calls=%async_computation.1 | async-start | bytes 2097152 | tf_op jit(solution)/shard_map/psum | solution.py:191
  316.5 1.4 copy-start.11
  316.5 1.4 copy-start.16
  317.9 12.0 %copy-start.15 = (f32[8,32,512]{2,1,0:T(8,128)S(1)}, f32[8,32,512]{2,1,0:T(8,128)}, u32[]{:S(2)}) copy-start(f32[8,32,512]{2,1,0:T(8,128)} %copy-done.14) | copy-start | bytes 1572868
  329.9 1.3 copy-start.17
  329.9 1.5 copy-start.18
Sparse Core Ops, SparseCore 0:
  257.6 58.8 all-reduce.10
  319.5 51.4 all-reduce.12
